TPU v7x, 32 devices: a whole 2x2x4 slice. The times are simulated.
32 devices in a mesh: dp: 16 (over z, x, core), tp: 2 (over y).
Axes of the slice: x: 2, y: 2, z: 4, core: 2. Of those that a mesh axis runs over, the one named last changes fastest.
Arguments:
- tokens: float32 [16384, 1024], P(('dp', 'tp')), may hold values from -6 to 6
- v_first: bfloat16 [16384, 1024], P('dp', 'tp'), may hold values from -6 to 6
- w_query: bfloat16 [1024, 1024], P(None, 'tp'), may hold values from -0.1875 to 0.1875
- w_key: bfloat16 [1024, 1024], P(None, 'tp'), may hold values from -0.1875 to 0.1875
- w_value: bfloat16 [1024, 1024], P(None, 'tp'), may hold values from -0.1875 to 0.1875
- w_out: bfloat16 [1024, 1024], P('tp'), may hold values from -3 to 3
- w_gate: bfloat16 [1024, 2816], P(None, 'tp'), may hold values from -0.1875 to 0.1875
- w_up: bfloat16 [1024, 2816], P(None, 'tp'), may hold values from -0.1875 to 0.1875
- w_down: bfloat16 [2816, 1024], P('tp'), may hold values from -0.109375 to 0.109375
- gain_attn: float32 [1024], replicated, may hold values from 0.5 to 1.5
- gain_mlp: float32 [1024], replicated, may hold values from 0.5 to 1.5
- seq_lens: int32 [16, 1], P('dp'), may hold values from 0 to 1024, as said below
- cotangent: float32 [16384, 1024], P(('dp', 'tp')), may hold values from -6 to 6
Outputs:
- layer_out: float32 [16384, 1024], P(('dp', 'tp'))
- grad_tokens: float32 [16384, 1024], P(('dp', 'tp'))
- grad_first: float32 [16384, 1024], P('dp', 'tp')
- grad_query: float32 [1024, 1024], P(None, 'tp')
- grad_key: float32 [1024, 1024], P(None, 'tp')
- grad_value: float32 [1024, 1024], P(None, 'tp')
- grad_output: float32 [1024, 1024], P('tp')
- grad_gate: float32 [1024, 2816], P(None, 'tp')
- grad_up: float32 [1024, 2816], P(None, 'tp')
- grad_down: float32 [2816, 1024], P('tp')
- grad_gain_attn: float32 [1024], replicated
- grad_gain_mlp: float32 [1024], replicated
Inputs may be any that keep to these rules, and one draw needn't show every extreme that they name: `seq_lens`: in each data group the nonzero lengths are 1024, 2048 or 4096 and all lengths sum to 1024; some group holds a sequence of the largest length.
All inputs are finite; a program needn't handle non-finite values.
Results may differ from a plain program's by a relative error of at most 0.02.
Values may be sent and summed in bfloat16 or wider, within the bound.
A program may use at most 192 MiB of HBM per device.

v0:
```python
import jax
import jax.numpy as jnp
from jax import lax
from jax.sharding import PartitionSpec as P

HDIM = 64


EPS = 1e-06


def layout(seq_row, row_share, tp_count):
    group_rows = row_share * tp_count
    row_ids = jnp.arange(group_rows, dtype=jnp.int32)
    device = row_ids // row_share
    local_row = row_ids % row_share
    pieces = seq_row // (2 * tp_count)
    slot_ends = jnp.cumsum(2 * pieces)
    starts = slot_ends - 2 * pieces
    offset = local_row[:, None] - starts[None, :]
    inside = (offset >= 0) & (offset < 2 * pieces[None, :])
    first_half = offset < pieces[None, :]
    mirror = 2 * tp_count - 1 - device[:, None]
    position = jnp.where(
        first_half,
        device[:, None] * pieces[None, :] + offset,
        mirror * pieces[None, :] + offset - pieces[None, :],
    )
    slot_ids = jnp.arange(seq_row.shape[0], dtype=jnp.int32)
    doc_ids = jnp.sum(jnp.where(inside, slot_ids[None, :], 0), axis=1)
    positions = jnp.sum(jnp.where(inside, position, 0), axis=1)
    return (doc_ids, positions)


def rotate(values, positions, head_dim, turn_sign):
    row_count, width_all = values.shape
    half_dim = head_dim // 2
    shaped = values.reshape(row_count, width_all // head_dim, head_dim)
    freqs = 10000.0 ** (-jnp.arange(half_dim, dtype=jnp.float32) / half_dim)
    angles = positions.astype(jnp.float32)[:, None] * freqs[None, :]
    cosine = jnp.cos(angles)[:, None, :]
    sine = turn_sign * jnp.sin(angles)[:, None, :]
    front = shaped[..., :half_dim]
    behind = shaped[..., half_dim:]
    turned = jnp.concatenate(
        [front * cosine - behind * sine, behind * cosine + front * sine], axis=-1
    )
    return turned.reshape(row_count, width_all)


def normalize(values, gain):
    return values * lax.rsqrt(jnp.mean(values * values, axis=-1, keepdims=True) + EPS) * gain


def normalize_back(values, gain, grad_in):
    factor = lax.rsqrt(jnp.mean(values * values, axis=-1, keepdims=True) + EPS)
    normed = values * factor
    grad_normed = grad_in * gain
    grad_values = factor * (
        grad_normed - normed * jnp.mean(grad_normed * normed, axis=-1, keepdims=True)
    )
    return (grad_values, jnp.sum(grad_in * normed, axis=0))


def inner_rows(left, right):
    return lax.dot_general(
        left, right, (((0,), (0,)), ((), ())), preferred_element_type=jnp.float32
    )


def outer_cols(left, right):
    return lax.dot_general(
        left, right, (((1,), (1,)), ((), ())), preferred_element_type=jnp.float32
    )


def swiglu_back(gate, up_values, grad_hidden):
    sigma = jax.nn.sigmoid(gate)
    grad_gate = grad_hidden * up_values * (sigma * (1.0 + gate * (1.0 - sigma)))
    grad_upper = grad_hidden * (gate * sigma)
    return (grad_gate.astype(jnp.bfloat16), grad_upper.astype(jnp.bfloat16))


def block_mask(doc_ids, positions, first_row, block_rows):
    row_doc = lax.dynamic_slice_in_dim(doc_ids, first_row, block_rows, 0)
    row_pos = lax.dynamic_slice_in_dim(positions, first_row, block_rows, 0)
    return (row_doc[:, None] == doc_ids[None, :]) & (positions[None, :] <= row_pos[:, None])


def attention_forward(query, keys, values, doc_ids, positions, head_dim):
    group_rows, width_local = query.shape
    head_count = width_local // head_dim
    block_rows = min(512, group_rows)
    block_count = group_rows // block_rows
    score_scale = head_dim ** (-0.5)
    key_heads = keys.reshape(group_rows, head_count, head_dim)
    value_heads = values.reshape(group_rows, head_count, head_dim)

    def forward_block(block_index):
        first_row = block_index * block_rows
        query_rows = lax.dynamic_slice_in_dim(query, first_row, block_rows, 0).reshape(
            block_rows, head_count, head_dim
        )
        scores = (
            jnp.einsum("qhd,khd->hqk", query_rows, key_heads, preferred_element_type=jnp.float32)
            * score_scale
        )
        allowed = block_mask(doc_ids, positions, first_row, block_rows)
        scores = jnp.where(allowed[None], scores, -1e30)
        row_max = jnp.max(scores, axis=-1, keepdims=True)
        exponent = jnp.exp(scores - row_max)
        row_total = jnp.sum(exponent, axis=-1, keepdims=True)
        weights = (exponent / row_total).astype(jnp.bfloat16)
        mixture = jnp.einsum(
            "hqk,khd->qhd", weights, value_heads, preferred_element_type=jnp.float32
        )
        return (
            mixture.astype(jnp.bfloat16).reshape(block_rows, width_local),
            (row_max + jnp.log(row_total))[..., 0],
        )

    mixture, row_lse = lax.map(forward_block, jnp.arange(block_count, dtype=jnp.int32))
    return (mixture.reshape(group_rows, width_local), row_lse)


def attention_backward(query, keys, values, grad_mixture, row_lse, doc_ids, positions, head_dim):
    group_rows, width_local = query.shape
    head_count = width_local // head_dim
    block_rows = min(512, group_rows)
    block_count = group_rows // block_rows
    score_scale = head_dim ** (-0.5)
    key_heads = keys.reshape(group_rows, head_count, head_dim)
    value_heads = values.reshape(group_rows, head_count, head_dim)

    def backward_block(carry, block_index):
        key_total, value_total = carry
        first_row = block_index * block_rows
        query_rows = lax.dynamic_slice_in_dim(query, first_row, block_rows, 0).reshape(
            block_rows, head_count, head_dim
        )
        grad_rows = lax.dynamic_slice_in_dim(grad_mixture, first_row, block_rows, 0).reshape(
            block_rows, head_count, head_dim
        )
        scores = (
            jnp.einsum("qhd,khd->hqk", query_rows, key_heads, preferred_element_type=jnp.float32)
            * score_scale
        )
        allowed = block_mask(doc_ids, positions, first_row, block_rows)
        scores = jnp.where(allowed[None], scores, -1e30)
        weights = jnp.exp(scores - row_lse[block_index][..., None])
        weights_low = weights.astype(jnp.bfloat16)
        grad_weights = jnp.einsum(
            "qhd,khd->hqk", grad_rows, value_heads, preferred_element_type=jnp.float32
        )
        weighted_sum = jnp.sum(weights * grad_weights, axis=-1, keepdims=True)
        score_grad = (weights * (grad_weights - weighted_sum)).astype(jnp.bfloat16)
        query_grad = (
            jnp.einsum("hqk,khd->qhd", score_grad, key_heads, preferred_element_type=jnp.float32)
            * score_scale
        )
        key_total = (
            key_total
            + jnp.einsum("hqk,qhd->khd", score_grad, query_rows, preferred_element_type=jnp.float32)
            * score_scale
        )
        value_total = value_total + jnp.einsum(
            "hqk,qhd->khd", weights_low, grad_rows, preferred_element_type=jnp.float32
        )
        return (
            (key_total, value_total),
            query_grad.astype(jnp.bfloat16).reshape(block_rows, width_local),
        )

    zero_heads = jnp.zeros((group_rows, head_count, head_dim), jnp.float32)
    (key_total, value_total), query_grad = lax.scan(
        backward_block, (zero_heads, zero_heads), jnp.arange(block_count, dtype=jnp.int32)
    )
    return (
        query_grad.reshape(group_rows, width_local),
        key_total.reshape(group_rows, width_local).astype(jnp.bfloat16),
        value_total.reshape(group_rows, width_local).astype(jnp.bfloat16),
    )


def local(
    tokens,
    v_first,
    w_query,
    w_key,
    w_value,
    w_out,
    w_gate,
    w_up,
    w_down,
    gain_attn,
    gain_mlp,
    seq_lens,
    cotangent,
):
    tp_count = lax.axis_size("tp")
    row_share = tokens.shape[0]
    doc_ids, positions = layout(seq_lens[0], row_share, tp_count)
    normed_attn = lax.all_gather(
        normalize(tokens, gain_attn).astype(jnp.bfloat16), "tp", axis=0, tiled=True
    )
    query = rotate(
        jnp.dot(normed_attn, w_query, preferred_element_type=jnp.float32), positions, HDIM, 1.0
    ).astype(jnp.bfloat16)
    keys = rotate(
        jnp.dot(normed_attn, w_key, preferred_element_type=jnp.float32), positions, HDIM, 1.0
    ).astype(jnp.bfloat16)
    value_pre = jnp.dot(normed_attn, w_value, preferred_element_type=jnp.float32)
    mixed_values = (0.5 * value_pre + 0.5 * v_first.astype(jnp.float32)).astype(jnp.bfloat16)
    attended, row_lse = attention_forward(query, keys, mixed_values, doc_ids, positions, HDIM)
    middle = tokens + lax.psum_scatter(
        jnp.dot(attended, w_out, preferred_element_type=jnp.float32),
        "tp",
        scatter_dimension=0,
        tiled=True,
    )
    normed_mlp = normalize(middle, gain_mlp).astype(jnp.bfloat16)
    grad_branch = cotangent.astype(jnp.bfloat16)
    mlp_rows = lax.all_gather(normed_mlp, "tp", axis=0, tiled=True)
    gate = jnp.dot(mlp_rows, w_gate, preferred_element_type=jnp.float32)
    up_values = jnp.dot(mlp_rows, w_up, preferred_element_type=jnp.float32)
    hidden = (jax.nn.silu(gate) * up_values).astype(jnp.bfloat16)
    layer_out = middle + lax.psum_scatter(
        jnp.dot(hidden, w_down, preferred_element_type=jnp.float32).astype(jnp.bfloat16),
        "tp",
        scatter_dimension=0,
        tiled=True,
    ).astype(jnp.float32)
    cot_rows = lax.all_gather(grad_branch, "tp", axis=0, tiled=True)
    grad_down = inner_rows(hidden, cot_rows)
    gate_grad, up_grad = swiglu_back(gate, up_values, outer_cols(cot_rows, w_down))
    grad_gate = inner_rows(mlp_rows, gate_grad)
    grad_up = inner_rows(mlp_rows, up_grad)
    grad_mlp_in = lax.psum_scatter(
        (outer_cols(gate_grad, w_gate) + outer_cols(up_grad, w_up)).astype(jnp.bfloat16),
        "tp",
        scatter_dimension=0,
        tiled=True,
    ).astype(jnp.float32)
    middle_back, grad_gain_mlp = normalize_back(middle, gain_mlp, grad_mlp_in)
    grad_middle = cotangent + middle_back
    attn_cot_rows = lax.all_gather(grad_middle.astype(jnp.bfloat16), "tp", axis=0, tiled=True)
    grad_output = inner_rows(attended, attn_cot_rows)
    grad_attended = outer_cols(attn_cot_rows, w_out).astype(jnp.bfloat16)
    query_grad, key_grad, mixed_grad = attention_backward(
        query, keys, mixed_values, grad_attended, row_lse, doc_ids, positions, HDIM
    )
    half_mixed = 0.5 * mixed_grad.astype(jnp.float32)
    value_grad = half_mixed.astype(jnp.bfloat16)
    query_pre_grad = rotate(query_grad.astype(jnp.float32), positions, HDIM, -1.0).astype(
        jnp.bfloat16
    )
    key_pre_grad = rotate(key_grad.astype(jnp.float32), positions, HDIM, -1.0).astype(jnp.bfloat16)
    grad_query = inner_rows(normed_attn, query_pre_grad)
    grad_key = inner_rows(normed_attn, key_pre_grad)
    grad_value = inner_rows(normed_attn, value_grad)
    grad_attn_in = lax.psum_scatter(
        (
            outer_cols(query_pre_grad, w_query)
            + outer_cols(key_pre_grad, w_key)
            + outer_cols(value_grad, w_value)
        ).astype(jnp.bfloat16),
        "tp",
        scatter_dimension=0,
        tiled=True,
    ).astype(jnp.float32)
    tokens_back, grad_gain_attn = normalize_back(tokens, gain_attn, grad_attn_in)
    grad_tokens = grad_middle + tokens_back
    grad_query, grad_key, grad_value, grad_output, grad_gate, grad_up, grad_down = (
        lax.psum(grad_query.astype(jnp.bfloat16), "dp").astype(jnp.float32),
        lax.psum(grad_key.astype(jnp.bfloat16), "dp").astype(jnp.float32),
        lax.psum(grad_value.astype(jnp.bfloat16), "dp").astype(jnp.float32),
        lax.psum(grad_output.astype(jnp.bfloat16), "dp").astype(jnp.float32),
        lax.psum(grad_gate.astype(jnp.bfloat16), "dp").astype(jnp.float32),
        lax.psum(grad_up.astype(jnp.bfloat16), "dp").astype(jnp.float32),
        lax.psum(grad_down.astype(jnp.bfloat16), "dp").astype(jnp.float32),
    )
    grad_gain_attn, grad_gain_mlp = lax.psum((grad_gain_attn, grad_gain_mlp), ("dp", "tp"))
    return (
        layer_out,
        grad_tokens,
        half_mixed,
        grad_query,
        grad_key,
        grad_value,
        grad_output,
        grad_gate,
        grad_up,
        grad_down,
        grad_gain_attn,
        grad_gain_mlp,
    )


def solution(mesh):
    in_specs = (
        P(("dp", "tp"), None),
        P("dp", "tp"),
        P(None, "tp"),
        P(None, "tp"),
        P(None, "tp"),
        P("tp", None),
        P(None, "tp"),
        P(None, "tp"),
        P("tp", None),
        P(),
        P(),
        P("dp", None),
        P(("dp", "tp"), None),
    )
    out_specs = (
        P(("dp", "tp"), None),
        P(("dp", "tp"), None),
        P("dp", "tp"),
        P(None, "tp"),
        P(None, "tp"),
        P(None, "tp"),
        P("tp", None),
        P(None, "tp"),
        P(None, "tp"),
        P("tp", None),
        P(),
        P(),
    )
    return jax.shard_map(local, mesh=mesh, in_specs=in_specs, out_specs=out_specs, check_vma=False)
```

profile of v0, /device:TPU:0, one launch (start us, length us, event | category | flops | bytes accessed | tf_op | source)
XLA Modules:
  0.0 809.0 jit_solution(9884071972371629396)
XLA Ops:
  15.3 31.7 %all-gather.5.cloned.1.call-done = bf16[1024,1024]{1,0:T(8,128)(2,1)} async-done(((bf16[512,1024]{1,0:T(8,128)(2,1)}), bf16[1024,1024]{1,0:T(8,128)(2,1)}) %all-gather.5.cloned.1.call-update) | async-done | bytes 2097168 | tf_op jit(solution)/shard_map/all_gather | solution.py:203
  57.0 36.4 %while.29 = (s32[]{:T(128)}, bf16[2,512,512]{2,1,0:T(8,128)(2,1)}, f32[2,8,512]{2,1,0:T(8,128)S(1)}, s32[1024]{0:T(1024)S(1)}, s32[2]{0:T(128)S(1)}, /*index=5*/...) while((s32[]{:T(128)}, bf16[2,512,512]{2,1,0:T(8,128)(2,1)}, ...), condition=%wide.region_4.5_spmd, body=%wide.region_1.4_spmd.sunk | while | flops 1124855808 | bytes 67250424 | solution.py:122
  62.9 4.2 fusion.128
  67.1 5.8 fusion.129
  85.2 5.8 fusion.129
  93.4 4.8 fusion.48
  98.3 54.4 %reduce-scatter.5.cloned.1.call-done = f32[512,1024]{1,0:T(8,128)} async-done(((f32[1024,1024]{1,0:T(8,128)}), f32[512,1024]{1,0:T(8,128)}) %reduce-scatter.5.cloned.1.call-update) | async-done | bytes 2097168 | tf_op jit(solution)/shard_map/reduce_scatter | solution.py:215
  160.6 30.4 %all-gather.7.cloned.1.call-done = bf16[1024,1024]{1,0:T(8,128)(2,1)} async-done(((bf16[512,1024]{1,0:T(8,128)(2,1)}), bf16[1024,1024]{1,0:T(8,128)(2,1)}) %all-gather.7.cloned.1.call-update) | async-done | bytes 2097168 | tf_op jit(solution)/shard_map/all_gather | solution.py:223
  191.0 8.5 %fusion.50 = f32[1024,1408]{1,0:T(8,128)} fusion(bf16[1024,1024]{1,0:T(8,128)(2,1)} %all-gather.7.cloned.1.call-done, bf16[1024,1408]{1,0:T(8,128)(2,1)} %param.24), kind=kOutput, calls=%fused_computation.118 | convolution fusion | flops 2952790016 | bytes 10747904 | tf_op jit(solution)/shard_map/dot_general | solution.py:225
  199.6 5.2 fusion.49
  204.8 21.5 %all-gather.9.cloned.1.call-done = bf16[1024,1024]{1,0:T(8,128)(2,1)} async-done(((bf16[512,1024]{1,0:T(8,128)(2,1)}), bf16[1024,1024]{1,0:T(8,128)(2,1)}) %all-gather.9.cloned.1.call-update) | async-done | bytes 2097168 | tf_op jit(solution)/shard_map/all_gather | solution.py:233
  226.3 10.2 %multiply_convert_fusion.1 = (bf16[1024,1408]{1,0:T(8,128)(2,1)S(1)}, bf16[1024,1408]{1,0:T(8,128)(2,1)S(1)}, bf16[1024,1408]{1,0:T(8,128)(2,1)}) fusion(f32[1024,1408]{1,0:T(8,128)} %fusion.49, f32[1024,1408]{1,0:T(8,128)} %fusion.50, bf16[1024,1024]{1,0:T(8,128)(2,1)} %all-gather.9.cloned.1.call-done, bf16[1408,1024]{1,0:T(8,128)(2,1)S(1)} %copy-done), kind=kOutput, calls=%fused_computation.27 | convolution fusion | flops 2974416896 | bytes 25165824 | tf_op jit(solution)/shard_map/dot_general | solution.py:72
  240.4 4.6 add_convert_fusion.1
  245.1 31.9 %reduce-scatter.9.cloned.1.call-done = bf16[512,1024]{1,0:T(8,128)(2,1)} async-done(((bf16[1024,1024]{1,0:T(8,128)(2,1)}), bf16[512,1024]{1,0:T(8,128)(2,1)}) %reduce-scatter.9.cloned.1.call-update) | async-done | bytes 1048592 | tf_op jit(solution)/shard_map/reduce_scatter | solution.py:238
  283.8 33.2 %all-gather.11.cloned.1.call-done = bf16[1024,1024]{1,0:T(8,128)(2,1)} async-done(((bf16[512,1024]{1,0:T(8,128)(2,1)}), bf16[1024,1024]{1,0:T(8,128)(2,1)}) %all-gather.11.cloned.1.call-update) | async-done | bytes 2097168 | tf_op jit(solution)/shard_map/all_gather | solution.py:246
  321.1 124.1 %while.30 = (s32[]{:T(128)}, f32[1024,8,64]{0,2,1:T(8,128)}, f32[1024,8,64]{0,2,1:T(8,128)}, bf16[2,512,512]{1,2,0:T(8,128)(2,1)}, s32[2]{0:T(128)S(1)}, /*index...) while((s32[]{:T(128)}, f32[1024,8,64]{0,2,1:T(8,128)}, ...), condition=%wide.region_12.13_spmd.clone, body=%wide.region_10.12_spmd.clone.sunk | while | flops 2725769216 | bytes 281635328 | solution.py:175
  329.9 8.2 %fusion.140 = f32[8,512,1024]{2,1,0:T(8,128)} fusion(bf16[512,8,64]{0,2,1:T(8,128)(2,1)S(1)} %bitcast.136, bf16[1024,8,64]{0,2,1:T(8,128)(2,1)S(1)} %copy-done.8), kind=kOutput, calls=%fused_computation.113.clone.1 | convolution fusion | flops 536870912 | bytes 18350080 | tf_op jit(solution)/shard_map/while/body/eval_jaxpr/qhd,khd->hqk/dot_general | solution.py:152
  338.1 12.7 %multiply_reduce_fusion.4 = (f32[8,512]{1,0:T(8,128)S(1)}, f32[8,512,1024]{2,1,0:T(8,128)}) fusion(f32[8,512,1024]{2,1,0:T(8,128)} %fusion.140, f32[8,512]{1,0:T(8,128)S(1)} %dynamic-slice_bitcast_fusion.2, bf16[512,8,64]{0,2,1:T(8,128)(2,1)S(1)} %bitcast.138, bf16[1024,8,64]{0,2,1:T(8,128)(2,1)S(1)} %copy-done.4, pred[512,1024]{1,0:T(8,128)(4,1)S(1)} %copy-done.10), kind=kOutput, calls=%fused_computation.14.clone.1 | convolution fusion | flops 557838336 | bytes 35684352 | tf_op jit(solution)/shard_map/while/body/eval_jaxpr/qhd,khd->hqk/dot_general | solution.py:145
  350.8 15.0 %multiply_convert_fusion.8 = bf16[8,512,1024]{2,1,0:T(8,128)(2,1)} fusion(f32[8,512,1024]{2,1,0:T(8,128)} %get-tuple-element.457, f32[8,512,1024]{2,1,0:T(8,128)} %fusion.140, f32[8,512]{1,0:T(8,128)S(1)} %get-tuple-element.458), kind=kLoop, calls=%fused_computation.13.clone.1 | loop fusion | flops 12582912 | bytes 41959424 | tf_op jit(solution)/shard_map/while/body/eval_jaxpr/convert_element_type | solution.py:156
  372.1 6.2 fusion.141
  391.0 8.2 %fusion.140 = f32[8,512,1024]{2,1,0:T(8,128)} fusion(bf16[512,8,64]{0,2,1:T(8,128)(2,1)S(1)} %bitcast.136, bf16[1024,8,64]{0,2,1:T(8,128)(2,1)S(1)} %copy-done.8), kind=kOutput, calls=%fused_computation.113.clone.1 | convolution fusion | flops 536870912 | bytes 18350080 | tf_op jit(solution)/shard_map/while/body/eval_jaxpr/qhd,khd->hqk/dot_general | solution.py:152
  399.2 12.6 %multiply_reduce_fusion.4 = (f32[8,512]{1,0:T(8,128)S(1)}, f32[8,512,1024]{2,1,0:T(8,128)}) fusion(f32[8,512,1024]{2,1,0:T(8,128)} %fusion.140, f32[8,512]{1,0:T(8,128)S(1)} %dynamic-slice_bitcast_fusion.2, bf16[512,8,64]{0,2,1:T(8,128)(2,1)S(1)} %bitcast.138, bf16[1024,8,64]{0,2,1:T(8,128)(2,1)S(1)} %copy-done.4, pred[512,1024]{1,0:T(8,128)(4,1)S(1)} %copy-done.10), kind=kOutput, calls=%fused_computation.14.clone.1 | convolution fusion | flops 557838336 | bytes 35684352 | tf_op jit(solution)/shard_map/while/body/eval_jaxpr/qhd,khd->hqk/dot_general | solution.py:145
  411.8 15.0 %multiply_convert_fusion.8 = bf16[8,512,1024]{2,1,0:T(8,128)(2,1)} fusion(f32[8,512,1024]{2,1,0:T(8,128)} %get-tuple-element.457, f32[8,512,1024]{2,1,0:T(8,128)} %fusion.140, f32[8,512]{1,0:T(8,128)S(1)} %get-tuple-element.458), kind=kLoop, calls=%fused_computation.13.clone.1 | loop fusion | flops 12582912 | bytes 41959424 | tf_op jit(solution)/shard_map/while/body/eval_jaxpr/convert_element_type | solution.py:156
  430.3 4.6 bitcast_add_fusion.5
  434.9 6.2 fusion.141
  466.9 6.4 convolution_convert_fusion.3
  473.4 7.4 convolution_convert_fusion
  480.8 5.1 convolution_convert_fusion.1
  486.0 4.9 convolution_convert_fusion.2
  505.6 40.5 %all-reduce = (f32[1024]{0:T(1024)}, f32[1024]{0:T(1024)}) all-reduce(f32[1024]{0:T(1024)S(1)} %get-tuple-element.258, f32[1024]{0:T(1024)S(1)} %copy-done.48), channel_id=1, replica_groups=mesh['dp'=16,'tp'=2] {'dp','tp'}, use_global_device_ids=true, to_apply=%region_23.24 | all-reduce | flops 2048 | bytes 16384 | tf_op jit(solution)/shard_map/psum | solution.py:282
  546.2 6.2 fusion.18
  552.3 231.7 %all-reduce.4.cloned.1.call-done = (bf16[1024,512]{1,0:T(8,128)(2,1)}, bf16[1024,512]{1,0:T(8,128)(2,1)}, bf16[1024,512]{1,0:T(8,128)(2,1)}, bf16[512,1024]{1,0:...) async-done(((bf16[1024,512]{1,0:T(8,128)(2,1)}, bf16[1024,512]{1,0:T(8,128)(2,1)}, bf16[1024,512]{1,0:T(8,128)(2,1)}, ...) | async-done | bytes 12845072 | tf_op jit(solution)/shard_map/psum | solution.py:274
  (257 shorter events, 143.7 us)
Async XLA Ops:
  7.2 219.1 %copy-start = (bf16[1408,1024]{1,0:T(8,128)(2,1)S(1)}, bf16[1408,1024]{1,0:T(8,128)(2,1)}, u32[]{:S(2)}) copy-start(bf16[1408,1024]{1,0:T(8,128)(2,1)} %param.25) | copy-start | bytes 8650756
  7.2 39.8 %all-gather.5.cloned.1.call-start = ((), (), s32[]{:S(2)}) async-start(), calls=%async_computation.4 | async-start | bytes 3145728 | tf_op jit(solution)/shard_map/all_gather | solution.py:203
  11.1 141.6 %reduce-scatter.5.cloned.1.call-start = ((), (), s32[]{:S(2)}) async-start(), calls=%async_computation.5 | async-start | bytes 6291456 | tf_op jit(solution)/shard_map/reduce_scatter | solution.py:215
  15.3 36.4 %copy-start.22 = (f32[1024,32]{0,1:T(8,128)}, f32[1024,32]{0,1:T(8,128)S(1)}, u32[]{:S(2)}) copy-start(f32[1024,32]{0,1:T(8,128)S(1)} %get-tuple-element.332) | copy-start | bytes 393220
  98.2 58.3 %copy-start.38 = (f32[1024]{0:T(1024)S(1)}, f32[1024]{0:T(1024)}, u32[]{:S(2)}) copy-start(f32[1024]{0:T(1024)} %param.27) | copy-start | bytes 12292
  98.2 92.8 %all-gather.7.cloned.1.call-start = ((), (), s32[]{:S(2)}) async-start(), calls=%async_computation.6 | async-start | bytes 3145728 | tf_op jit(solution)/shard_map/all_gather | solution.py:223
  155.2 125.2 %copy-start.40 = (f32[512]{0:T(512)}, f32[512]{0:T(512)S(1)}, u32[]{:S(2)}) copy-start(f32[512]{0:T(512)S(1)} %add_rsqrt_fusion) | copy-start | bytes 6148
  157.8 68.5 %all-gather.9.cloned.1.call-start = ((), (), s32[]{:S(2)}) async-start(), calls=%async_computation.8 | async-start | bytes 3145728 | tf_op jit(solution)/shard_map/all_gather | solution.py:233
  160.6 116.5 %reduce-scatter.9.cloned.1.call-start = ((), (), s32[]{:S(2)}) async-start(), calls=%async_computation.9 | async-start | bytes 3145728 | tf_op jit(solution)/shard_map/reduce_scatter | solution.py:238
  191.0 8.5 %copy-start.49 = (bf16[1024,1408]{1,0:T(8,128)(2,1)S(1)}, bf16[1024,1408]{1,0:T(8,128)(2,1)}, u32[]{:S(2)}) copy-start(bf16[1024,1408]{1,0:T(8,128)(2,1)} %param.23) | copy-start | bytes 8650756
  191.0 8.5 %copy-start.54 = (bf16[1024,1024]{1,0:T(8,128)(2,1)S(1)}, bf16[1024,1024]{1,0:T(8,128)(2,1)}, u32[]{:S(2)}) copy-start(bf16[1024,1024]{1,0:T(8,128)(2,1)} %all-gather.7.cloned.1.call-done) | copy-start | bytes 6291460
  226.2 10.3 %copy-start.50 = (bf16[1024,1408]{1,0:T(8,128)(2,1)S(1)}, bf16[1024,1408]{1,0:T(8,128)(2,1)}, u32[]{:S(2)}) copy-start(bf16[1024,1408]{1,0:T(8,128)(2,1)} %param.23) | copy-start | bytes 8650756
  245.1 71.9 %all-gather.11.cloned.1.call-start = ((), (), s32[]{:S(2)}) async-start(), calls=%async_computation.10 | async-start | bytes 3145728 | tf_op jit(solution)/shard_map/all_gather | solution.py:246
  283.7 219.2 %reduce-scatter.11.cloned.1.call-start = ((), (), s32[]{:S(2)}) async-start(), calls=%async_computation.11 | async-start | bytes 3145728 | tf_op jit(solution)/shard_map/reduce_scatter | solution.py:261
  329.9 8.2 %copy-start.4 = (bf16[1024,8,64]{0,2,1:T(8,128)(2,1)S(1)}, bf16[1024,8,64]{0,2,1:T(8,128)(2,1)}, u32[]{:S(2)}) copy-start(bf16[1024,8,64]{0,2,1:T(8,128)(2,1)} %get-tuple-element.534) | copy-start | bytes 3145732 | tf_op jit(solution)/shard_map/while
  329.9 8.2 %copy-start.10 = (pred[512,1024]{1,0:T(8,128)(4,1)S(1)}, pred[512,1024]{1,0:T(8,128)(4,1)}, u32[]{:S(2)}) copy-start(pred[512,1024]{1,0:T(8,128)(4,1)} %broadcast_compare_fusion.5) | copy-start | bytes 1572868 | tf_op jit(solution)/shard_map/while
  350.7 18.4 %copy-start.1 = (f32[8,512,1024]{2,1,0:T(8,128)S(1)}, f32[8,512,1024]{2,1,0:T(8,128)}, u32[]{:S(2)}) copy-start(f32[8,512,1024]{2,1,0:T(8,128)} %get-tuple-element.457) | copy-start | bytes 50331652 | tf_op jit(solution)/shard_map/while
  369.2 9.1 %copy-start.5 = (f32[1024,8,64]{0,2,1:T(8,128)S(1)}, f32[1024,8,64]{0,2,1:T(8,128)}, u32[]{:S(2)}) copy-start(f32[1024,8,64]{0,2,1:T(8,128)} %get-tuple-element.512) | copy-start | bytes 6291460 | tf_op jit(solution)/shard_map/while
  372.1 6.2 copy-start.2
  391.0 8.2 %copy-start.4 = (bf16[1024,8,64]{0,2,1:T(8,128)(2,1)S(1)}, bf16[1024,8,64]{0,2,1:T(8,128)(2,1)}, u32[]{:S(2)}) copy-start(bf16[1024,8,64]{0,2,1:T(8,128)(2,1)} %get-tuple-element.534) | copy-start | bytes 3145732 | tf_op jit(solution)/shard_map/while
  391.0 8.2 %copy-start.10 = (pred[512,1024]{1,0:T(8,128)(4,1)S(1)}, pred[512,1024]{1,0:T(8,128)(4,1)}, u32[]{:S(2)}) copy-start(pred[512,1024]{1,0:T(8,128)(4,1)} %broadcast_compare_fusion.5) | copy-start | bytes 1572868 | tf_op jit(solution)/shard_map/while
  411.8 18.4 %copy-start.1 = (f32[8,512,1024]{2,1,0:T(8,128)S(1)}, f32[8,512,1024]{2,1,0:T(8,128)}, u32[]{:S(2)}) copy-start(f32[8,512,1024]{2,1,0:T(8,128)} %get-tuple-element.457) | copy-start | bytes 50331652 | tf_op jit(solution)/shard_map/while
  430.2 10.8 %copy-start.5 = (f32[1024,8,64]{0,2,1:T(8,128)S(1)}, f32[1024,8,64]{0,2,1:T(8,128)}, u32[]{:S(2)}) copy-start(f32[1024,8,64]{0,2,1:T(8,128)} %get-tuple-element.512) | copy-start | bytes 6291460 | tf_op jit(solution)/shard_map/while
  434.9 6.2 copy-start.2
  455.4 8.7 %copy-start.14 = (f32[1024,8,64]{0,2,1:T(8,128)}, f32[1024,8,64]{0,2,1:T(8,128)S(1)}, u32[]{:S(2)}) copy-start(f32[1024,8,64]{0,2,1:T(8,128)S(1)} %convert_multiply_fusion.4) | copy-start | bytes 6291460
  466.9 79.3 %reduce-scatter.7.cloned.1.call-start = ((), (), s32[]{:S(2)}) async-start(), calls=%async_computation.7 | async-start | bytes 3145728 | tf_op jit(solution)/shard_map/reduce_scatter | solution.py:227
  473.4 310.6 %all-reduce.4.cloned.1.call-start = ((), (), s32[]{:S(2)}) async-start(), calls=%async_computation.12 | async-start | bytes 25690112 | tf_op jit(solution)/shard_map/psum | solution.py:274
  473.4 7.4 copy-start.55
  473.4 7.4 copy-start.62
  502.9 43.2 %copy-start.39 = (f32[1024]{0:T(1024)S(1)}, f32[1024]{0:T(1024)}, u32[]{:S(2)}) copy-start(f32[1024]{0:T(1024)} %param.27) | copy-start | bytes 12292
  502.9 43.3 %copy-start.41 = (f32[512]{0:T(512)S(1)}, f32[512]{0:T(512)}, u32[]{:S(2)}) copy-start(f32[512]{0:T(512)} %copy-done.40) | copy-start | bytes 6148
  502.9 43.3 %copy-start.47 = (f32[512]{0:T(512)S(1)}, f32[512]{0:T(512)}, u32[]{:S(2)}) copy-start(f32[512]{0:T(512)} %copy-done.46) | copy-start | bytes 6148
  (51 other events, 127.8 us)
Sparse Core Ops, SparseCore 0:
  11.2 35.8 all-gather.4
  98.4 54.2 reduce-scatter.4
  157.9 33.1 all-gather.6
  193.1 33.1 all-gather.8
  245.2 31.8 reduce-scatter.8
  283.8 33.1 all-gather.10
  467.0 31.8 reduce-scatter.10
  501.8 32.5 reduce-scatter.6
  541.0 242.9 all-reduce.3
where the time goes:
time: 819 us; the launch traced here: 809 us
  waiting for transfers between devices  435 us (53%)
  matrix products  169 us (21%)
  other arithmetic  89.9 us (11%)
  local copies, waits for them, and re-layouts  52.2 us (6%)
  blocking collectives  40.5 us (5%)
  between operations  15.5 us (2%)
    psum x1, waiting for transfers between devices, local(): lax.psum(grad_query.astype(jnp.bfloat16), 'dp').astype(jnp.float32)  232 us
    reduce_scatter x1, waiting for transfers between devices, local(): lax.psum_scatter(jnp.dot(attended, w_out, preferred_element_type=jnp.floa...  54.4 us
    psum x1, blocking collectives, local(): lax.psum((grad_gain_attn, grad_gain_mlp), ('dp', 'tp'))  40.5 us
    all_gather x1, waiting for transfers between devices, local(): lax.all_gather(grad_middle.astype(jnp.bfloat16), 'tp', axis=0, tiled=True)  33.2 us
    reduce_scatter x1, waiting for transfers between devices, local(): lax.psum_scatter((outer_cols(gate_grad, w_gate) + outer_cols(up_grad, w_u...  31.9 us
    all_gather x1, waiting for transfers between devices, local(): lax.all_gather(normalize(tokens, gain_attn).astype(jnp.bfloat16), 'tp', a...  31.7 us
    all_gather x1, waiting for transfers between devices, local(): mlp_rows = lax.all_gather(normed_mlp, 'tp', axis=0, tiled=True)  30.4 us
    convert_element_type x2, other arithmetic, backward_block(): score_grad = (weights * (grad_weights - weighted_sum)).astype(jnp.bfloat16)  30 us
  transfers between devices with their start and end apart: 9, of which 7 were waited for; matrix products, arithmetic and copies ran while one was open for 8% of the time, Pallas kernels for 0%

commit v1 on v0

--- a/solution.py
+++ b/solution.py
@@ -1,6 +1,11 @@
+import functools
+
 import jax
 import jax.numpy as jnp
+import numpy as np
 from jax import lax
+from jax.experimental import pallas as pl
+from jax.experimental.pallas import tpu as pltpu
 from jax.sharding import PartitionSpec as P
 
 HDIM = 64
@@ -180,6 +185,239 @@
         key_total.reshape(group_rows, width_local).astype(jnp.bfloat16),
         value_total.reshape(group_rows, width_local).astype(jnp.bfloat16),
     )
+
+
+BF, F32 = jnp.bfloat16, jnp.float32
+BLK = 256
+POS_OF = (0, 3, 1, 2)
+NT = (((1,), (1,)), ((), ()))
+
+def nt(a, b):
+    return lax.dot_general(a, b, NT, preferred_element_type=F32)
+
+def nn(a, b):
+    return jnp.dot(a, b, preferred_element_type=F32)
+
+def rows(block):
+    return pl.ds(block * BLK, BLK)
+
+def turn(u, cosine, sine, lane):
+    near = jnp.where(lane % 64 < 32, pltpu.roll(u, 96, 1), pltpu.roll(u, 32, 1))
+    return u * cosine + near * sine
+
+def fwd_kernel(x_ref, wq_ref, wk_ref, wv_ref, vf_ref, cos_ref, sin_ref,
+               q_ref, k_ref, v_ref, o_ref, lse_ref, vt_ref):
+    lane = lax.broadcasted_iota(jnp.int32, (BLK, 128), 1)
+    for m in range(4):
+        at = rows(POS_OF[m])
+        x = x_ref[rows(m), :]
+        cosine, sine = cos_ref[rows(m), :], sin_ref[rows(m), :]
+        qf, kf = nn(x, wq_ref[...]), nn(x, wk_ref[...])
+        vf = 0.5 * nn(x, wv_ref[...]) + 0.5 * vf_ref[rows(m), :].astype(F32)
+        for t in range(2):
+            cols = slice(t * 128, t * 128 + 128)
+            q_ref[at, cols] = turn(qf[:, cols], cosine, sine, lane).astype(BF) * 0.125
+            k_ref[at, cols] = turn(kf[:, cols], cosine, sine, lane).astype(BF)
+        low = vf.astype(BF)
+        v_ref[at, :] = low
+        vt_ref[:, at] = low.T
+    lse_ref[...] = jnp.zeros_like(lse_ref)
+    causal = lax.broadcasted_iota(jnp.int32, (BLK, BLK), 0) <= lax.broadcasted_iota(jnp.int32, (BLK, BLK), 1)
+    for t in range(2):
+        cols = slice(t * 128, t * 128 + 128)
+        for m in range(4):
+            i = POS_OF[m]
+            n = BLK * (i + 1)
+            q = q_ref[rows(i), cols]
+            parts = []
+            for h in range(2):
+                qm = jnp.where((lane < 64) == (h == 0), q, jnp.zeros_like(q))
+                scores = [nt(k_ref[rows(j), cols], qm) for j in range(i + 1)]
+                scores[i] = jnp.where(causal, scores[i], -1e30)
+                top = functools.reduce(jnp.maximum, [jnp.max(s, axis=0, keepdims=True) for s in scores])
+                es = [jnp.exp(s - top) for s in scores]
+                total = functools.reduce(jnp.add, [jnp.sum(e, axis=0, keepdims=True) for e in es])
+                head = slice(t * 128 + h * 64, t * 128 + h * 64 + 64)
+                ot = functools.reduce(jnp.add, [nn(vt_ref[head, rows(j)], es[j].astype(BF)) for j in range(i + 1)])
+                parts.append(ot * (1.0 / total))
+                lse_ref[t * 2 + h : t * 2 + h + 1, rows(i)] = top + jnp.log(total)
+            o_ref[rows(m), cols] = jnp.concatenate(parts, axis=0).T.astype(BF)
+
+def attn_fwd(x, wq, wk, wv, vf, cos, sin):
+    R = 1024
+    full = lambda s: pl.BlockSpec(s, lambda g: (0, 0))
+    col = pl.BlockSpec((R, 256), lambda g: (0, g))
+    return pl.pallas_call(
+        fwd_kernel, grid=(2,),
+        in_specs=[full((R, 1024)), col, col, col, col, full((R, 128)), full((R, 128))],
+        out_specs=[col, col, col, col, pl.BlockSpec((None, 8, R), lambda g: (g, 0, 0))],
+        out_shape=[jax.ShapeDtypeStruct((R, 512), BF)] * 4 + [jax.ShapeDtypeStruct((2, 8, R), F32)],
+        scratch_shapes=[pltpu.VMEM((256, R), BF)],
+        compiler_params=pltpu.CompilerParams(vmem_limit_bytes=50 << 20),
+        cost_estimate=pl.CostEstimate(flops=10 * 10**9, bytes_accessed=12 << 20, transcendentals=5 << 20),
+    )(x, wq, wk, wv, vf, cos, sin)
+
+def bwd_kernel(c_ref, wo_ref, q_ref, k_ref, v_ref, o_ref, lse_ref, cos_ref, sin_ref,
+               dq_ref, dk_ref, dv_ref, gf_ref, do_ref, kt_ref, dka_ref, dva_ref, dl_ref):
+    lane = lax.broadcasted_iota(jnp.int32, (BLK, 128), 1)
+    for m in range(4):
+        at = rows(POS_OF[m])
+        low = nt(c_ref[rows(m), :], wo_ref[...]).astype(BF)
+        do_ref[at, :] = low
+        prod = (low.astype(F32) * o_ref[rows(m), :].astype(F32)).T
+        for h in range(4):
+            dl_ref[h : h + 1, at] = jnp.sum(prod[h * 64 : h * 64 + 64, :], axis=0, keepdims=True)
+        kt_ref[:, at] = k_ref[at, :].T
+    causal = lax.broadcasted_iota(jnp.int32, (BLK, BLK), 0) <= lax.broadcasted_iota(jnp.int32, (BLK, BLK), 1)
+    for t in range(2):
+        cols = slice(t * 128, t * 128 + 128)
+        for m in range(4):
+            i = POS_OF[m]
+            q, do = q_ref[rows(i), cols], do_ref[rows(i), cols]
+            parts = []
+            for h in range(2):
+                mine = (lane < 64) == (h == 0)
+                qm = jnp.where(mine, q, jnp.zeros_like(q))
+                dom = jnp.where(mine, do, jnp.zeros_like(do))
+                lse = lse_ref[t * 2 + h : t * 2 + h + 1, rows(i)]
+                delta = dl_ref[t * 2 + h : t * 2 + h + 1, rows(i)]
+                head = slice(t * 128 + h * 64, t * 128 + h * 64 + 64)
+                dqt = None
+                for j in range(i + 1):
+                    p = jnp.exp(nt(k_ref[rows(j), cols], qm) - lse)
+                    if j == i:
+                        p = jnp.where(causal, p, 0.0)
+                    ds = (p * (nt(v_ref[rows(j), cols], dom) - delta)).astype(BF)
+                    dv, dk = nn(p.astype(BF), dom), nn(ds, qm)
+                    dva_ref[rows(j), cols] = dv if (m, h) == FIRST[j] else dva_ref[rows(j), cols] + dv
+                    dka_ref[rows(j), cols] = dk if (m, h) == FIRST[j] else dka_ref[rows(j), cols] + dk
+                    part = nn(kt_ref[head, rows(j)], ds)
+                    dqt = part if dqt is None else dqt + part
+                parts.append(dqt)
+            dq = (jnp.concatenate(parts, axis=0).T * 0.125).astype(BF).astype(F32)
+            dq_ref[rows(m), cols] = turn(dq, cos_ref[rows(m), :], -sin_ref[rows(m), :], lane).astype(BF)
+    for m in range(4):
+        at = rows(POS_OF[m])
+        cosine, sine = cos_ref[rows(m), :], -sin_ref[rows(m), :]
+        for t in range(2):
+            cols = slice(t * 128, t * 128 + 128)
+            dk = dka_ref[at, cols].astype(BF).astype(F32)
+            dk_ref[rows(m), cols] = turn(dk, cosine, sine, lane).astype(BF)
+        half = 0.5 * dva_ref[at, :].astype(BF).astype(F32)
+        dv_ref[rows(m), :] = half.astype(BF)
+        gf_ref[rows(m), :] = half
+
+FIRST = {}
+for _m in range(4):
+    for _j in range(POS_OF[_m] + 1):
+        FIRST.setdefault(_j, (_m, 0))
+
+def attn_bwd(c, wo, q, k, v, o, lse, cos, sin):
+    R = 1024
+    full = lambda s: pl.BlockSpec(s, lambda g: (0, 0))
+    col = pl.BlockSpec((R, 256), lambda g: (0, g))
+    return pl.pallas_call(
+        bwd_kernel, grid=(2,),
+        in_specs=[full((R, 1024)), pl.BlockSpec((256, 1024), lambda g: (g, 0)), col, col, col, col,
+                  pl.BlockSpec((None, 8, R), lambda g: (g, 0, 0)), full((R, 128)), full((R, 128))],
+        out_specs=[col] * 4,
+        out_shape=[jax.ShapeDtypeStruct((R, 512), BF)] * 3 + [jax.ShapeDtypeStruct((R, 512), F32)],
+        scratch_shapes=[pltpu.VMEM((R, 256), BF), pltpu.VMEM((256, R), BF), pltpu.VMEM((R, 256), F32),
+                        pltpu.VMEM((R, 256), F32), pltpu.VMEM((8, R), F32)],
+        compiler_params=pltpu.CompilerParams(vmem_limit_bytes=50 << 20),
+        cost_estimate=pl.CostEstimate(flops=20 * 10**9, bytes_accessed=12 << 20, transcendentals=5 << 20),
+    )(c, wo, q, k, v, o, lse, cos, sin)
+
+def tables():
+    pos = np.zeros(1024, np.float32)
+    for m in range(4):
+        pos[m*256:(m+1)*256] = POS_OF[m]*256 + np.arange(256)
+    freqs = np.float32(10000.0) ** (-np.arange(32, dtype=np.float32) / np.float32(32))
+    ang = pos[:, None] * freqs[None]
+    c, s = np.cos(ang.astype(np.float32)), np.sin(ang.astype(np.float32))
+    return np.tile(c, (1, 4)).astype(np.float32), np.concatenate([-s, s, -s, s], 1).astype(np.float32)
+
+def swap(block):
+    return lax.ppermute(block, "tp", [(0, 1), (1, 0)])
+
+
+def joined(mine, other):
+    pair = jnp.concatenate([mine, other], axis=0)
+    return jnp.where(lax.axis_index("tp") == 0, pair, jnp.roll(pair, mine.shape[0], axis=0))
+
+
+def local_pair(
+    tokens,
+    v_first,
+    w_query,
+    w_key,
+    w_value,
+    w_out,
+    w_gate,
+    w_up,
+    w_down,
+    gain_attn,
+    gain_mlp,
+    seq_lens,
+    cotangent,
+):
+    row_share = tokens.shape[0]
+    me = lax.axis_index("tp")
+    cosine, sine = tables()
+    own = lambda whole: lax.dynamic_slice_in_dim(whole, me * row_share, row_share, 0)
+    theirs = lambda whole: lax.dynamic_slice_in_dim(whole, (1 - me) * row_share, row_share, 0)
+
+    def scatter(partial):
+        return own(partial) + swap(theirs(partial).astype(jnp.bfloat16)).astype(jnp.float32)
+
+    def gather(mine):
+        return joined(mine, swap(mine))
+
+    normed_attn = gather(normalize(tokens, gain_attn).astype(jnp.bfloat16))
+    query, keys, mixed_values, attended, row_lse = attn_fwd(
+        normed_attn, w_query, w_key, w_value, v_first, cosine, sine
+    )
+    middle = tokens + scatter(jnp.dot(attended, w_out, preferred_element_type=jnp.float32))
+    mlp_rows = gather(normalize(middle, gain_mlp).astype(jnp.bfloat16))
+    cot_rows = gather(cotangent.astype(jnp.bfloat16))
+    gate = jnp.dot(mlp_rows, w_gate, preferred_element_type=jnp.float32)
+    up_values = jnp.dot(mlp_rows, w_up, preferred_element_type=jnp.float32)
+    hidden = (jax.nn.silu(gate) * up_values).astype(jnp.bfloat16)
+    layer_out = middle + scatter(jnp.dot(hidden, w_down, preferred_element_type=jnp.float32))
+    gate_grad, up_grad = swiglu_back(gate, up_values, outer_cols(cot_rows, w_down))
+    grad_mlp_in = scatter(outer_cols(gate_grad, w_gate) + outer_cols(up_grad, w_up))
+    grad_down = inner_rows(hidden, cot_rows)
+    grad_gate = inner_rows(mlp_rows, gate_grad)
+    grad_up = inner_rows(mlp_rows, up_grad)
+    grad_gate, grad_up, grad_down = lax.psum(
+        tuple(g.astype(jnp.bfloat16) for g in (grad_gate, grad_up, grad_down)), "dp"
+    )
+    middle_back, grad_gain_mlp = normalize_back(middle, gain_mlp, grad_mlp_in)
+    grad_middle = cotangent + middle_back
+    attn_cot_rows = gather(grad_middle.astype(jnp.bfloat16))
+    query_pre_grad, key_pre_grad, value_grad, grad_first = attn_bwd(
+        attn_cot_rows, w_out, query, keys, mixed_values, attended, row_lse, cosine, sine
+    )
+    grad_attn_in = scatter(
+        outer_cols(query_pre_grad, w_query)
+        + outer_cols(key_pre_grad, w_key)
+        + outer_cols(value_grad, w_value)
+    )
+    grad_output = inner_rows(attended, attn_cot_rows)
+    grad_query = inner_rows(normed_attn, query_pre_grad)
+    grad_key = inner_rows(normed_attn, key_pre_grad)
+    grad_value = inner_rows(normed_attn, value_grad)
+    tokens_back, grad_gain_attn = normalize_back(tokens, gain_attn, grad_attn_in)
+    grad_tokens = grad_middle + tokens_back
+    grad_query, grad_key, grad_value, grad_output = lax.psum(
+        tuple(g.astype(jnp.bfloat16) for g in (grad_query, grad_key, grad_value, grad_output)), "dp"
+    )
+    grad_gain_attn, grad_gain_mlp = lax.psum((grad_gain_attn, grad_gain_mlp), ("dp", "tp"))
+    wide = [
+        g.astype(jnp.float32)
+        for g in (grad_query, grad_key, grad_value, grad_output, grad_gate, grad_up, grad_down)
+    ]
+    return (layer_out, grad_tokens, grad_first, *wide, grad_gain_attn, grad_gain_mlp)
 
 
 def local(
@@ -326,4 +564,10 @@
         P(),
         P(),
     )
-    return jax.shard_map(local, mesh=mesh, in_specs=in_specs, out_specs=out_specs, check_vma=False)
+
+    def step(*args):
+        tokens, seq_lens = args[0], args[11]
+        pair = mesh.shape["tp"] == 2 and seq_lens.shape[1] == 1 and tokens.shape == (512, 1024)
+        return (local_pair if pair else local)(*args)
+
+    return jax.shard_map(step, mesh=mesh, in_specs=in_specs, out_specs=out_specs, check_vma=False)

time: 819 us -> 546 us (0.67)
  waiting for transfers between devices: 435 us -> 310 us
  matrix products: 169 us -> 73.6 us
  other arithmetic: 89.9 us -> 38 us
  local copies, waits for them, and re-layouts: 52.2 us -> 4.95 us
  Pallas kernels: 0 us -> 43.9 us
  starting transfers between devices: 0.37 us -> 11 us
    ppermute x0 -> x8, waiting for transfers between devices: none -> 138 us  [swap(): return lax.ppermute(block, 'tp', [(0, 1), (1, 0)])]
    all_gather x4 -> x0, waiting for transfers between devices: 117 us -> none  [the longest x1 33.2 us: local(): lax.all_gather(grad_middle.astype(jnp.bfloat16), 'tp', axis=0, tiled=True)]
    dot_general x21 -> x4, matrix products: 115 us -> 20.8 us  [the longest x1 7.28 us: local_pair(): gate = jnp.dot(mlp_rows, w_gate, preferred_element_type=jnp.float32)]
    reduce_scatter x4 -> x0, waiting for transfers between devices: 86.4 us -> none  [the longest x1 54.4 us: local(): lax.psum_scatter(jnp.dot(attended, w_out, preferred_element_type=jnp.floa...]
    psum x1, waiting for transfers between devices: 232 us -> 172 us  [local_pair(): lax.psum(tuple((g.astype(jnp.bfloat16) for g in (grad_query, grad_key, gr...]
    pallas_call x0 -> x2, Pallas kernels: none -> 43.9 us  [the longest x1 24.9 us: attn_bwd(): pl.pallas_call(bwd_kernel, grid=(2,), in_specs=[full((R, 1024)), pl.Block...]
    convert_element_type x15 -> x11, other arithmetic: 57.2 us -> 21.4 us  [the longest x7 16.8 us: local_pair(): g.astype(jnp.float32)]
    dynamic_slice x16 -> x0, local copies, waits for them, and re-layouts: 13.4 us -> none  [the longest x4 6.28 us: backward_block(): lax.dynamic_slice_in_dim(grad_mixture, first_row, block_rows, 0)]
  transfers between devices with their start and end apart: 9 -> 9, of which waited for: 7 -> 9; matrix products, arithmetic and copies ran while one was open for 8% -> 9% of each run, Pallas kernels for 0% -> 0%
where the time goes in v1:
time: 546 us; the launch traced here: 536 us
  waiting for transfers between devices  310 us (57%)
  matrix products  73.6 us (13%)
  Pallas kernels  43.9 us (8%)
  blocking collectives  40.3 us (7%)
  other arithmetic  38 us (7%)
  between operations  14.9 us (3%)
  starting transfers between devices  11 us (2%)
    psum x1, waiting for transfers between devices, local_pair(): lax.psum(tuple((g.astype(jnp.bfloat16) for g in (grad_query, grad_key, gr...  172 us
    ppermute x8, waiting for transfers between devices, swap(): return lax.ppermute(block, 'tp', [(0, 1), (1, 0)])  138 us
    psum x1, blocking collectives, local_pair(): lax.psum((grad_gain_attn, grad_gain_mlp), ('dp', 'tp'))  40.3 us
    dot_general x6, matrix products, outer_cols(): lax.dot_general(left, right, (((1,), (1,)), ((), ())), preferred_element_...  26.6 us
    dot_general x7, matrix products, inner_rows(): lax.dot_general(left, right, (((0,), (0,)), ((), ())), preferred_element_...  26.2 us
    pallas_call x1, Pallas kernels, attn_bwd(): pl.pallas_call(bwd_kernel, grid=(2,), in_specs=[full((R, 1024)), pl.Block...  24.9 us
    pallas_call x1, Pallas kernels, attn_fwd(): pl.pallas_call(fwd_kernel, grid=(2,), in_specs=[full((R, 1024)), col, col...  19 us
    convert_element_type x7, other arithmetic, local_pair(): g.astype(jnp.float32)  16.8 us
  transfers between devices with their start and end apart: 9, of which 9 were waited for; matrix products, arithmetic and copies ran while one was open for 9% of the time, Pallas kernels for 0%

profile of v1, /device:TPU:0, one launch (start us, length us, event | category | flops | bytes accessed | tf_op | source)
XLA Modules:
  0.0 536.4 jit_solution(14578205212764409738)
XLA Ops:
  10.8 3.0 collective-permute-start
  13.8 23.5 %collective-permute-done = bf16[512,1024]{1,0:T(8,128)(2,1)} collective-permute-done((bf16[512,1024]{1,0:T(8,128)(2,1)}, bf16[512,1024]{1,0:T(8,128)(2,1)}, u32[]{:S(2)}, u32[]{:S(2)}) %collective-permute-start) | collective-permute-done | bytes 1048608 | tf_op jit(solution)/shard_map/ppermute | solution.py:341
  37.2 4.7 maximum_select_fusion.x_ref
  41.9 19.0 %shard_map.229 = (bf16[1024,512]{1,0:T(8,128)(2,1)S(1)}, bf16[1024,512]{1,0:T(8,128)(2,1)S(1)}, bf16[1024,512]{1,0:T(8,128)(2,1)}, bf16[1024,512]{1,0:T(8,128)(2,1)}, f32[2,8,1024]{2,1,0:T(8,128)S(1)}) custom-call(bf16[1024,1024]{1,0:T(8,128)(2,1)} %maximum_select_fusion.x_ref, bf16[1024,512]{1,0:T(8,128)(2,1)} %wq_ref.1, bf16[1024,512]{1,0:T(8,128)(2,1)} %wk_ref.1, ...), custom_call_target="tpu_custom_call" | custom-call | flops 10000000000 | bytes 12582912 | tf_op jit(solution)/shard_map/pallas_call | solution.py:250
  60.9 3.2 fusion.7
  68.3 22.9 %collective-permute-done.1 = bf16[512,1024]{1,0:T(8,128)(2,1)} collective-permute-done((bf16[512,1024]{1,0:T(8,128)(2,1)}, bf16[512,1024]{1,0:T(8,128)(2,1)}, u32[]{:S(2)}, u32[]{:S(2)}) %collective-permute-start.1) | collective-permute-done | bytes 1048608 | tf_op jit(solution)/shard_map/ppermute | solution.py:341
  91.2 3.0 multiply_reduce_fusion.4
  97.4 23.2 %collective-permute-done.2 = bf16[512,1024]{1,0:T(8,128)(2,1)S(1)} collective-permute-done((bf16[512,1024]{1,0:T(8,128)(2,1)S(1)}, bf16[512,1024]{1,0:T(8,128)(2,1)S(1)}, u32[]{:S(2)}, u32[]{:S(2)}) %collective-permute-start.2) | collective-permute-done | bytes 1048608 | tf_op jit(solution)/shard_map/ppermute | solution.py:341
  120.6 6.8 %fusion.4 = f32[1024,1408]{1,0:T(8,128)} fusion(bf16[1024,1408]{1,0:T(8,128)(2,1)S(1)} %copy-done.28, bf16[512,1024]{1,0:T(8,128)(2,1)S(1)} %collective-permute-done.2, bf16[512,1024]{1,0:T(8,128)(2,1)S(1)} %multiply_convert_fusion.3, pred[]{:T(512)S(6)} %eq.2), kind=kOutput, calls=%fused_computation.43 | convolution fusion | flops 2962227200 | bytes 10747905 | tf_op jit(solution)/shard_map/dot_general | solution.py:384
  127.4 7.3 %fusion.5 = f32[1024,1408]{1,0:T(8,128)} fusion(bf16[1024,1408]{1,0:T(8,128)(2,1)S(1)} %copy-done.27, bf16[512,1024]{1,0:T(8,128)(2,1)S(1)} %collective-permute-done.2, bf16[512,1024]{1,0:T(8,128)(2,1)S(1)} %multiply_convert_fusion.3, pred[]{:T(512)S(6)} %eq.2), kind=kOutput, calls=%fused_computation.44 | convolution fusion | flops 2962227200 | bytes 10747905 | tf_op jit(solution)/shard_map/dot_general | solution.py:383
  134.7 5.7 %collective-permute-done.4 = bf16[512,1024]{1,0:T(8,128)(2,1)S(1)} collective-permute-done((bf16[512,1024]{1,0:T(8,128)(2,1)S(1)}, bf16[512,1024]{1,0:T(8,128)(2,1)S(1)}, u32[]{:S(2)}, u32[]{:S(2)}) %collective-permute-start.4) | collective-permute-done | bytes 1048608 | tf_op jit(solution)/shard_map/ppermute | solution.py:341
  140.4 12.6 %multiply_convert_fusion = (bf16[1024,1408]{1,0:T(8,128)(2,1)}, bf16[1024,1408]{1,0:T(8,128)(2,1)}, bf16[1024,1408]{1,0:T(8,128)(2,1)}) fusion(f32[1024,1408]{1,0:T(8,128)} %fusion.5, f32[1024,1408]{1,0:T(8,128)} %fusion.4, bf16[1408,1024]{1,0:T(8,128)(2,1)S(1)} %copy-done, bf16[512,1024]{1,0:T(8,128)(2,1)S(1)} %collective-permute-done.4, ...), kind=kOutput, calls=%fused_computation | convolution fusion | flops 2983854080 | bytes 25165824 | tf_op jit(solution)/shard_map/dot_general | solution.py:77
  153.1 5.4 %fusion.9 = f32[1024,1024]{1,0:T(8,128)S(1)} fusion(bf16[1024,1408]{1,0:T(8,128)(2,1)} %get-tuple-element.48, bf16[1024,1408]{1,0:T(8,128)(2,1)S(1)} %copy-done.27), kind=kOutput, calls=%fused_computation.48 | convolution fusion | flops 2952790016 | bytes 9961472 | tf_op jit(solution)/shard_map/dot_general | solution.py:77
  158.5 3.4 convolution_add_fusion
  163.3 3.4 fusion.8
  167.9 5.2 convolution_convert_fusion.1
  173.1 15.2 %collective-permute-done.5 = bf16[512,1024]{1,0:T(8,128)(2,1)S(1)} collective-permute-done((bf16[512,1024]{1,0:T(8,128)(2,1)S(1)}, bf16[512,1024]{1,0:T(8,128)(2,1)S(1)}, u32[]{:S(2)}, u32[]{:S(2)}) %collective-permute-start.5) | collective-permute-done | bytes 1048608 | tf_op jit(solution)/shard_map/ppermute | solution.py:341
  189.0 18.1 %collective-permute-done.3 = bf16[512,1024]{1,0:T(8,128)(2,1)S(1)} collective-permute-done((bf16[512,1024]{1,0:T(8,128)(2,1)S(1)}, bf16[512,1024]{1,0:T(8,128)(2,1)S(1)}, u32[]{:S(2)}, u32[]{:S(2)}) %collective-permute-start.3) | collective-permute-done | bytes 1048608 | tf_op jit(solution)/shard_map/ppermute | solution.py:341
  207.2 3.0 fusion.6
  210.9 7.2 %convolution_convert_fusion.2 = bf16[1024,1408]{1,0:T(8,128)(2,1)} fusion(bf16[1024,1408]{1,0:T(8,128)(2,1)} %get-tuple-element.48, bf16[512,1024]{1,0:T(8,128)(2,1)S(1)} %collective-permute-done.2, bf16[512,1024]{1,0:T(8,128)(2,1)S(1)} %multiply_convert_fusion.3, pred[]{:T(512)S(6)} %eq.2), kind=kOutput, calls=%fused_computation.8 | convolution fusion | flops 2963668992 | bytes 7864321 | tf_op jit(solution)/shard_map/dot_general | solution.py:71
  218.1 4.7 convolution_convert_fusion
  222.8 8.9 %collective-permute-done.6 = bf16[512,1024]{1,0:T(8,128)(2,1)S(1)} collective-permute-done((bf16[512,1024]{1,0:T(8,128)(2,1)S(1)}, bf16[512,1024]{1,0:T(8,128)(2,1)S(1)}, u32[]{:S(2)}, u32[]{:S(2)}) %collective-permute-start.6) | collective-permute-done | bytes 1048608 | tf_op jit(solution)/shard_map/ppermute | solution.py:341
  235.1 24.9 %shard_map.230 = (bf16[1024,512]{1,0:T(8,128)(2,1)S(1)}, bf16[1024,512]{1,0:T(8,128)(2,1)S(1)}, bf16[1024,512]{1,0:T(8,128)(2,1)}, f32[1024,512]{1,0:T(8,128)}) custom-call(bf16[1024,1024]{1,0:T(8,128)(2,1)} %copy-done.11, bf16[512,1024]{1,0:T(8,128)(2,1)} %wo_ref.1, bf16[1024,512]{1,0:T(8,128)(2,1)} %copy-done.5, bf16[1024,512]{1,0:T(8,128)(2,1)} %copy-done.6, ...), custom_call_target="tpu_custom_call" | custom-call | flops 20000000000 | bytes 12582912 | tf_op jit(solution)/shard_map/pallas_call | solution.py:319
  266.9 2.6 fusion.11
  273.1 20.2 %collective-permute-done.7 = bf16[512,1024]{1,0:T(8,128)(2,1)S(1)} collective-permute-done((bf16[512,1024]{1,0:T(8,128)(2,1)S(1)}, bf16[512,1024]{1,0:T(8,128)(2,1)S(1)}, u32[]{:S(2)}, u32[]{:S(2)}) %collective-permute-start.7) | collective-permute-done | bytes 1048608 | tf_op jit(solution)/shard_map/ppermute | solution.py:341
  294.2 40.3 %all-reduce = (f32[1024]{0:T(1024)}, f32[1024]{0:T(1024)}) all-reduce(f32[1024]{0:T(1024)S(1)} %get-tuple-element.32, f32[1024]{0:T(1024)S(1)} %get-tuple-element.30), channel_id=1, replica_groups=mesh['dp'=16,'tp'=2] {'dp','tp'}, use_global_device_ids=true, to_apply=%region_12.13 | all-reduce | flops 2048 | bytes 16384 | tf_op jit(solution)/shard_map/psum | solution.py:415
  334.5 4.5 multiply_add_fusion
  339.0 172.1 %all-reduce.4.cloned.1.call-done = (bf16[1024,512]{1,0:T(8,128)(2,1)}, bf16[1024,512]{1,0:T(8,128)(2,1)}, bf16[1024,512]{1,0:T(8,128)(2,1)}, bf16[512,1024]{1,0:...) async-done(((bf16[1024,512]{1,0:T(8,128)(2,1)}, bf16[1024,512]{1,0:T(8,128)(2,1)}, bf16[1024,512]{1,0:T(8,128)(2,1)}, ...) | async-done | bytes 12845072 | tf_op jit(solution)/shard_map/psum | solution.py:412
  511.1 2.9 convert_element_type.103
  519.8 2.9 convert_element_type.111
  522.8 2.9 convert_element_type.113
  525.8 3.2 convert_element_type.115
  (107 shorter events, 35.6 us)
Async XLA Ops:
  7.2 133.2 %copy-start = (bf16[1408,1024]{1,0:T(8,128)(2,1)S(1)}, bf16[1408,1024]{1,0:T(8,128)(2,1)}, u32[]{:S(2)}) copy-start(bf16[1408,1024]{1,0:T(8,128)(2,1)} %param.23) | copy-start | bytes 8650756
  7.2 503.9 %all-reduce.4.cloned.1.call-start = ((), (), s32[]{:S(2)}) async-start(), calls=%async_computation | async-start | bytes 25690112 | tf_op jit(solution)/shard_map/psum | solution.py:412
  10.8 26.4 %collective-permute-start = (bf16[512,1024]{1,0:T(8,128)(2,1)}, bf16[512,1024]{1,0:T(8,128)(2,1)}, u32[]{:S(2)}, u32[]{:S(2)}) collective-permute-start(bf16[512,1024]{1,0:T(8,128)(2,1)} %multiply_convert_fusion.4), channel_id=1, source_target_pairs={{0,1},{1,0},{2,3},{3,2},{4,5},{5,4},{6,7},{7,6},{8,9},{9,8},{10,11... | collective-permute-start | bytes 3145736 | tf_op jit(solution)/shard_map/ppermute | solution.py:341
  13.8 28.2 %copy-start.2 = (f32[1024,128]{1,0:T(8,128)S(1)}, f32[1024,128]{1,0:T(8,128)}, u32[]{:S(2)}) copy-start(f32[1024,128]{1,0:T(8,128)} %constant.31.clone.sin_ref) | copy-start | bytes 1572868
  13.8 28.2 %copy-start.3 = (f32[1024,128]{1,0:T(8,128)S(1)}, f32[1024,128]{1,0:T(8,128)}, u32[]{:S(2)}) copy-start(f32[1024,128]{1,0:T(8,128)} %constant.30.clone.cos_ref) | copy-start | bytes 1572868
  41.9 19.0 %copy-start.30 = (bf16[512,1024]{1,0:T(8,128)(2,1)S(1)}, bf16[512,1024]{1,0:T(8,128)(2,1)}, u32[]{:S(2)}) copy-start(bf16[512,1024]{1,0:T(8,128)(2,1)} %wo_ref.1) | copy-start | bytes 3145732
  60.9 3.3 copy-start.5
  60.9 3.3 copy-start.6
  66.5 24.7 %collective-permute-start.1 = (bf16[512,1024]{1,0:T(8,128)(2,1)}, bf16[512,1024]{1,0:T(8,128)(2,1)}, u32[]{:S(2)}, u32[]{:S(2)}) collective-permute-start(bf16[512,1024]{1,0:T(8,128)(2,1)} %dynamic-slice_convert_fusion.3), channel_id=1, source_target_pairs={{0,1},{1,0},{2,3},{3,2},{4,5},{5,4},{6,7},{7,6},{8,9},{9,8},{10,11... | collective-permute-start | bytes 3145736 | tf_op jit(solution)/shard_map/ppermute | solution.py:341
  68.3 25.9 %copy-start.25 = (f32[1024]{0:T(1024)S(1)}, f32[1024]{0:T(1024)}, u32[]{:S(2)}) copy-start(f32[1024]{0:T(1024)} %param.25) | copy-start | bytes 12292
  94.4 26.2 %copy-start.28 = (bf16[1024,1408]{1,0:T(8,128)(2,1)S(1)}, bf16[1024,1408]{1,0:T(8,128)(2,1)}, u32[]{:S(2)}) copy-start(bf16[1024,1408]{1,0:T(8,128)(2,1)} %param.22) | copy-start | bytes 8650756
  94.5 26.2 %collective-permute-start.2 = (bf16[512,1024]{1,0:T(8,128)(2,1)S(1)}, bf16[512,1024]{1,0:T(8,128)(2,1)S(1)}, u32[]{:S(2)}, u32[]{:S(2)}) collective-permute-start(bf16[512,1024]{1,0:T(8,128)(2,1)S(1)} %multiply_convert_fusion.3), channel_id=1, source_target_pairs={{0,1},{1,0},{2,3},{3,2},{4,5},{5,4},{6,7},{7,6},{8,9},{9,8},{10,11... | collective-permute-start | bytes 3145736 | tf_op jit(solution)/shard_map/ppermute | solution.py:341
  96.1 31.3 %copy-start.27 = (bf16[1024,1408]{1,0:T(8,128)(2,1)S(1)}, bf16[1024,1408]{1,0:T(8,128)(2,1)}, u32[]{:S(2)}) copy-start(bf16[1024,1408]{1,0:T(8,128)(2,1)} %param.21) | copy-start | bytes 8650756
  96.1 44.3 %collective-permute-start.4 = (bf16[512,1024]{1,0:T(8,128)(2,1)S(1)}, bf16[512,1024]{1,0:T(8,128)(2,1)S(1)}, u32[]{:S(2)}, u32[]{:S(2)}) collective-permute-start(bf16[512,1024]{1,0:T(8,128)(2,1)S(1)} %convert_element_type.94), channel_id=1, source_target_pairs={{0,1},{1,0},{2,3},{3,2},{4,5},{5,4},{6,7},{7,6},{8,9},{9,8},{10,11... | collective-permute-start | bytes 3145736 | tf_op jit(solution)/shard_map/ppermute | solution.py:341
  140.4 12.6 %copy-start.32 = (bf16[512,1024]{1,0:T(8,128)(2,1)}, bf16[512,1024]{1,0:T(8,128)(2,1)S(1)}, u32[]{:S(2)}) copy-start(bf16[512,1024]{1,0:T(8,128)(2,1)S(1)} %collective-permute-done.4) | copy-start | bytes 3145732
  153.0 5.4 %copy-start.29 = (bf16[1024,1408]{1,0:T(8,128)(2,1)S(1)}, bf16[1024,1408]{1,0:T(8,128)(2,1)}, u32[]{:S(2)}) copy-start(bf16[1024,1408]{1,0:T(8,128)(2,1)} %param.22) | copy-start | bytes 8650756
  153.0 5.4 %copy-start.36 = (bf16[1024,1408]{1,0:T(8,128)(2,1)S(1)}, bf16[1024,1408]{1,0:T(8,128)(2,1)}, u32[]{:S(2)}) copy-start(bf16[1024,1408]{1,0:T(8,128)(2,1)} %get-tuple-element.47) | copy-start | bytes 8650756
  158.5 4.8 copy-start.34
  162.1 26.2 %collective-permute-start.5 = (bf16[512,1024]{1,0:T(8,128)(2,1)S(1)}, bf16[512,1024]{1,0:T(8,128)(2,1)S(1)}, u32[]{:S(2)}, u32[]{:S(2)}) collective-permute-start(bf16[512,1024]{1,0:T(8,128)(2,1)S(1)} %dynamic-slice_convert_fusion.1), channel_id=1, source_target_pairs={{0,1},{1,0},{2,3},{3,2},{4,5},{5,4},{6,7},{7,6},{8,9},{9,8},{10,11... | collective-permute-start | bytes 3145736 | tf_op jit(solution)/shard_map/ppermute | solution.py:341
  166.9 40.3 %collective-permute-start.3 = (bf16[512,1024]{1,0:T(8,128)(2,1)S(1)}, bf16[512,1024]{1,0:T(8,128)(2,1)S(1)}, u32[]{:S(2)}, u32[]{:S(2)}) collective-permute-start(bf16[512,1024]{1,0:T(8,128)(2,1)S(1)} %dynamic-slice_convert_fusion.2), channel_id=1, source_target_pairs={{0,1},{1,0},{2,3},{3,2},{4,5},{5,4},{6,7},{7,6},{8,9},{9,8},{10,11... | collective-permute-start | bytes 3145736 | tf_op jit(solution)/shard_map/ppermute | solution.py:341
  210.1 8.0 %copy-start.33 = (bf16[512,1024]{1,0:T(8,128)(2,1)S(1)}, bf16[512,1024]{1,0:T(8,128)(2,1)}, u32[]{:S(2)}) copy-start(bf16[512,1024]{1,0:T(8,128)(2,1)} %copy-done.32) | copy-start | bytes 3145732
  210.1 8.0 %copy-start.35 = (bf16[1024,1408]{1,0:T(8,128)(2,1)S(1)}, bf16[1024,1408]{1,0:T(8,128)(2,1)}, u32[]{:S(2)}) copy-start(bf16[1024,1408]{1,0:T(8,128)(2,1)} %get-tuple-element.49) | copy-start | bytes 8650756
  210.1 21.6 %collective-permute-start.6 = (bf16[512,1024]{1,0:T(8,128)(2,1)S(1)}, bf16[512,1024]{1,0:T(8,128)(2,1)S(1)}, u32[]{:S(2)}, u32[]{:S(2)}) collective-permute-start(bf16[512,1024]{1,0:T(8,128)(2,1)S(1)} %get-tuple-element.43), channel_id=1, source_target_pairs={{0,1},{1,0},{2,3},{3,2},{4,5},{5,4},{6,7},{7,6},{8,9},{9,8},{10,11... | collective-permute-start | bytes 3145736 | tf_op jit(solution)/shard_map/ppermute | solution.py:341
  222.8 9.9 %copy-start.24 = (bf16[1024,512]{1,0:T(8,128)(2,1)S(1)}, bf16[1024,512]{1,0:T(8,128)(2,1)}, u32[]{:S(2)}) copy-start(bf16[1024,512]{1,0:T(8,128)(2,1)} %get-tuple-element.21.o_ref) | copy-start | bytes 3145732
  235.1 25.0 %copy-start.17 = (bf16[1024,1024]{1,0:T(8,128)(2,1)S(1)}, bf16[1024,1024]{1,0:T(8,128)(2,1)}, u32[]{:S(2)}) copy-start(bf16[1024,1024]{1,0:T(8,128)(2,1)} %maximum_select_fusion.x_ref) | copy-start | bytes 6291460
  272.3 21.7 %copy-start.9 = (f32[1024,1024]{1,0:T(8,128)}, f32[1024,1024]{1,0:T(8,128)S(1)}, u32[]{:S(2)}) copy-start(f32[1024,1024]{1,0:T(8,128)S(1)} %add_add_fusion) | copy-start | bytes 12582916
  272.3 20.9 %copy-start.8 = (f32[512,1024]{1,0:T(8,128)S(1)}, f32[512,1024]{1,0:T(8,128)}, u32[]{:S(2)}) copy-start(f32[512,1024]{1,0:T(8,128)} %param.15) | copy-start | bytes 6291460
  272.5 20.7 %collective-permute-start.7 = (bf16[512,1024]{1,0:T(8,128)(2,1)S(1)}, bf16[512,1024]{1,0:T(8,128)(2,1)S(1)}, u32[]{:S(2)}, u32[]{:S(2)}) collective-permute-start(bf16[512,1024]{1,0:T(8,128)(2,1)S(1)} %dynamic-slice_convert_fusion), channel_id=1, source_target_pairs={{0,1},{1,0},{2,3},{3,2},{4,5},{5,4},{6,7},{7,6},{8,9},{9,8},{10,11... | collective-permute-start | bytes 3145736 | tf_op jit(solution)/shard_map/ppermute | solution.py:341
  511.1 2.9 copy-start.23
  519.8 3.0 copy-start.14
  522.8 3.0 copy-start.13
  525.8 3.3 copy-start.1
  (14 other events, 27.6 us)
Sparse Core Ops, SparseCore 0:
  267.0 244.0 all-reduce.3
